TPU v7x, 512 devices: a whole 4x8x8 slice. The times are simulated.
512 devices in a mesh: mode: 16 (over y_hi, x), resp: 16 (over z, y_lo), dof: 2 (over core).
Axes of the slice: x: 4, y: 8 (y_hi: 4, y_lo: 2; y = y_hi * 2 + y_lo), z: 8, core: 2. Of those that a mesh axis runs over, the one named last changes fastest.
Arguments:
- modes: bfloat16 [24576, 2048], P(('mode', 'dof')), may hold values from -0.0390625 to 0.0390625
- pressure: bfloat16 [24576, 2, 4096], P(('mode', 'dof'), None, 'resp'), may hold values from -6 to 6
- tile_list: int32 [640, 2], replicated, may hold values from 0 to 63, as said below
- slab_map: int32 [1024], replicated, may hold values from 0 to 1023, as said below
Outputs:
- forces: float32 [2048, 2, 4096], P(('mode', 'dof'), None, 'resp')
Inputs may be any that keep to these rules, and one draw needn't show every extreme that they name: `tile_list`: column 0 is below 16, column 1 below 64; rows may repeat. `slab_map`: blocks q * 32 to q * 32 + 31 form DOF group q; the slab blocks that a group takes come one from each DOF group, and every slab block is taken once.
All inputs are finite; a program needn't handle non-finite values.
Results may differ from a plain program's by a relative error of at most 0.0003.
Values may be sent and summed in bfloat16 or wider, within the bound.
A program may use at most 64 MiB of HBM per device.

v0:
```python
import jax
import jax.numpy as jnp
from jax import lax
from jax.sharding import PartitionSpec as P

MB = 128
RB = 64


def on_device(modes, pressure, tile_list, slab_map):
    group_size = lax.axis_size(("mode", "dof"))
    own_index = lax.axis_index(("mode", "dof"))
    dof_rows = pressure.shape[0]
    resp_cols = pressure.shape[2]
    block_rows = dof_rows // group_size
    table = slab_map.reshape(group_size, group_size)
    source = table // group_size
    offset = table % group_size
    send_index = jnp.sum(jnp.where(source == own_index, offset, 0), axis=1)
    blocks = pressure.reshape(group_size, block_rows, 2 * resp_cols)
    outgoing = jnp.take(blocks, send_index, axis=0)
    received = lax.all_to_all(outgoing, ("mode", "dof"), split_axis=0, concat_axis=0, tiled=True)
    own_source = lax.dynamic_index_in_dim(source, own_index, 0, keepdims=False)
    aligned = jnp.take(received, own_source, axis=0).reshape(dof_rows, 2 * resp_cols)
    local_blocks = resp_cols // RB
    resp_first = lax.axis_index("resp") * local_blocks
    mode_column = tile_list[:, 0]
    resp_column = tile_list[:, 1]
    mode_block = (
        lax.iota(jnp.int32, lax.axis_size(("mode", "dof")) * (modes.shape[1] // group_size)) // MB
    )
    resp_block = resp_first + lax.iota(jnp.int32, local_blocks)
    matched = (mode_column[None, None, :] == mode_block[:, None, None]) & (
        resp_column[None, None, :] == resp_block[None, :, None]
    )
    listed = jnp.any(matched, axis=2).astype(jnp.float32)
    column_mask = jnp.repeat(listed, RB, axis=1)
    column_mask = jnp.concatenate([column_mask, column_mask], axis=1)
    product = lax.dot_general(
        modes, aligned, (((0,), (0,)), ((), ())), preferred_element_type=jnp.float32
    )
    forces = lax.psum_scatter(
        product * column_mask, ("mode", "dof"), scatter_dimension=0, tiled=True
    )
    return forces.reshape(forces.shape[0], 2, resp_cols)


def solution(mesh):
    return jax.shard_map(
        on_device,
        mesh=mesh,
        in_specs=(P(("mode", "dof"), None), P(("mode", "dof"), None, "resp"), P(), P()),
        out_specs=P(("mode", "dof"), None, "resp"),
        check_vma=False,
    )
```

profile of v0, /device:TPU:1, one launch (start us, length us, event | category | flops | bytes accessed | tf_op | source)
XLA Modules:
  0.0 178.2 jit_solution(5088131174124574729)
XLA Ops:
  6.5 0.0 copy-start
  6.5 0.0 copy-start.1
  6.5 0.9 reshape.106
  7.5 0.1 add_select_fusion.1
  7.6 3.1 %reshape.105 = bf16[32,24,512]{2,1,0:T(8,128)(2,1)} reshape(bf16[768,2,256]{2,1,0:T(2,128)(2,1)} %param.7) | data formatting | bytes 1572864 | tf_op jit(solution)/shard_map/reshape | solution.py:20
  10.8 2.6 %gather_fusion = bf16[32,24,512]{2,1,0:T(8,128)(2,1)} fusion(bf16[32,24,512]{2,1,0:T(8,128)(2,1)} %reshape.105, s32[1024]{0:T(1024)S(1)} %pad_clamp_fusion.1), kind=kCustom, calls=%fused_computation.clone | custom fusion | bytes 1572992 | tf_op jit(solution)/shard_map/jit(_take)/gather | solution.py:21
  13.4 2.2 %broadcast_select_fusion.1 = bf16[32,24,512]{2,1,0:T(8,128)(2,1)} fusion(bf16[32,24,512]{2,1,0:T(8,128)(2,1)} %gather_fusion, pred[32]{0:T(512)(128)(4,1)S(1)} %compare_and_fusion.1), kind=kLoop, calls=%fused_computation.6 | loop fusion | flops 393216 | bytes 1572896 | tf_op jit(solution)/shard_map/jit(_take)/select_n | solution.py:21
  15.6 11.3 %all-to-all-start = ((bf16[32,24,512]{2,1,0:T(8,128)(2,1)}), bf16[32,24,512]{2,1,0:T(8,128)(2,1)}, u32[]{:S(2)}, u32[]{:S(2)}) async-start(bf16[32,24,512]{2,1,0:T(8,128)(2,1)} %broadcast_select_fusion.1), calls=%async_computation | async-start | bytes 1572864 | tf_op jit(solution)/shard_map/all_to_all | solution.py:22
  26.8 0.0 reduce-scatter.4.cloned.1.call-start
  26.9 0.0 copy-done.1
  27.0 0.1 broadcast_compare_fusion.1
  27.0 0.9 broadcast_compare_fusion
  27.9 1.8 %and_reduce_fusion = pred[2048,4]{0,1:T(4,128)(4,1)S(1)} fusion(pred[4,640]{1,0:T(4,128)(4,1)S(1)} %broadcast_compare_fusion.1, pred[2048,640]{1,0:T(8,128)(4,1)S(1)} %broadcast_compare_fusion), kind=kLoop, calls=%fused_computation.2 | loop fusion | flops 10477568 | bytes 1321472 | tf_op jit(solution)/shard_map/reduce_or | solution.py:36
  29.8 20.5 %all-to-all-done = bf16[32,24,512]{2,1,0:T(8,128)(2,1)} async-done(((bf16[32,24,512]{2,1,0:T(8,128)(2,1)}), bf16[32,24,512]{2,1,0:T(8,128)(2,1)}, u32[]{:S(2)}, u32[]{:S(2)}) %all-to-all-start) | async-done | bytes 786464 | tf_op jit(solution)/shard_map/all_to_all | solution.py:22
  50.3 2.6 %gather_fusion.1 = bf16[32,24,512]{2,1,0:T(8,128)(2,1)} fusion(bf16[32,24,512]{2,1,0:T(8,128)(2,1)} %all-to-all-done, s32[1024]{0:T(1024)S(1)} %pad_clamp_fusion), kind=kCustom, calls=%fused_computation.1.clone | custom fusion | bytes 1572992 | tf_op jit(solution)/shard_map/jit(_take)/gather | solution.py:24
  52.9 1.3 broadcast_select_fusion
  54.2 0.2 broadcast_in_dim.16
  54.4 0.0 copy-done
  54.4 4.0 %maximum_multiply_fusion = f32[2048,512]{0,1:T(8,128)} fusion(f32[2048,256]{0,1:T(8,128)S(1)} %bitcast.11, bf16[768,512]{1,0:T(8,128)(2,1)S(1)} %bitcast.13, bf16[768,2048]{1,0:T(8,128)(2,1)S(1)} %copy-done), kind=kOutput, calls=%fused_computation.3 | convolution fusion | flops 1612709888 | bytes 10223616 | tf_op jit(solution)/shard_map/dot_general | solution.py:39
  58.4 5.3 %copy.8 = f32[2048,512]{1,0:T(8,128)} copy(f32[2048,512]{0,1:T(8,128)} %maximum_multiply_fusion) | data formatting | bytes 8388608
  63.8 0.0 reduce-scatter.4.cloned.1.call-update
  63.8 105.7 %reduce-scatter.4.cloned.1.call-done = f32[64,512]{1,0:T(8,128)} async-done(((f32[2048,512]{1,0:T(8,128)}), f32[64,512]{1,0:T(8,128)}) %reduce-scatter.4.cloned.1.call-update) | async-done | bytes 131088
  169.5 1.0 copy.9
  170.6 0.8 copy.7
  (9 shorter events, 0.1 us)
Async XLA Ops:
  6.5 47.9 %copy-start = (bf16[768,2048]{1,0:T(8,128)(2,1)S(1)}, bf16[768,2048]{1,0:T(8,128)(2,1)}, u32[]{:S(2)}) copy-start(bf16[768,2048]{1,0:T(8,128)(2,1)} %param.6) | copy-start | bytes 9437188
  6.5 20.4 %copy-start.1 = (s32[640,2]{0,1:T(2,128)S(1)}, s32[640,2]{0,1:T(2,128)}, u32[]{:S(2)}) copy-start(s32[640,2]{0,1:T(2,128)} %param.8) | copy-start | bytes 15364
  15.6 34.7 %all-to-all-start = ((bf16[32,24,512]{2,1,0:T(8,128)(2,1)}), bf16[32,24,512]{2,1,0:T(8,128)(2,1)}, u32[]{:S(2)}, u32[]{:S(2)}) async-start(bf16[32,24,512]{2,1,0:T(8,128)(2,1)} %broadcast_select_fusion.1), calls=%async_computation | async-start | bytes 1572864 | tf_op jit(solution)/shard_map/all_to_all | solution.py:22
  26.8 142.7 %reduce-scatter.4.cloned.1.call-start = ((), (), s32[]{:S(2)}) async-start(), calls=%async_computation.2 | async-start | bytes 4325376
Sparse Core Ops, SparseCore 0:
  63.9 105.5 reduce-scatter.3
where the time goes:
time: 179 us; the launch traced here: 178 us
  waiting for transfers between devices  126 us (70%)
  local copies, waits for them, and re-layouts  16.7 us (9%)
  between operations  13.5 us (8%)
  starting transfers between devices  11.3 us (6%)
  other arithmetic  6.41 us (4%)
  matrix products  3.97 us (2%)
    unnamed x2, waiting for transfers between devices  106 us
    all_to_all x1, waiting for transfers between devices, on_device(): lax.all_to_all(outgoing, ('mode', 'dof'), split_axis=0, concat_axis=0, ti...  20.5 us
    all_to_all x1, starting transfers between devices, on_device(): lax.all_to_all(outgoing, ('mode', 'dof'), split_axis=0, concat_axis=0, ti...  11.3 us
    unnamed x6, local copies, waits for them, and re-layouts  6.38 us
    dot_general x1, matrix products, on_device(): lax.dot_general(modes, aligned, (((0,), (0,)), ((), ())), preferred_eleme...  3.97 us
  transfers between devices with their start and end apart: 2, of which 2 were waited for; matrix products, arithmetic and copies ran while one was open for 2% of the time, Pallas kernels for 0%

commit v1 on v0

v1 whole, which is shorter than its diff:
```python
import functools

import jax
import jax.numpy as jnp
from jax import lax
from jax.experimental import pallas as pl
from jax.experimental.pallas import tpu as pltpu
from jax.sharding import PartitionSpec as P

F32 = jnp.float32
BF16 = jnp.bfloat16
I16 = jnp.int16
LANES = 128
BROWS = 24
GROUP = 32
CHIPS = 16
TOP = 32760.0
STEP = 64.0


def encode(v):
    r = v.shape[0]
    v3 = v.reshape(r // 16, 16, LANES)
    top = jnp.maximum(jnp.max(jnp.abs(v3), axis=0), 2.0**-110)
    e = jnp.ceil(jnp.log2(top) * STEP)
    inv = jnp.exp2(e * (-1.0 / STEP)) * TOP
    code = jnp.round(v3 * inv[None]).astype(jnp.int32).reshape(r, LANES)
    return jnp.concatenate([code, e.astype(jnp.int32)], axis=0).astype(I16)


def decode(q):
    r = q.shape[0] - 16
    w = q.astype(jnp.int32).astype(F32)
    scale = jnp.exp2(w[r:] * (1.0 / STEP)) * (1.0 / TOP)
    return (w[:r].reshape(r // 16, 16, LANES) * scale[None]).reshape(r, LANES)


def kernel(
    slab,
    tiles,
    press_hbm,
    modes_hbm,
    out,
    press,
    modes,
    perm,
    sendb,
    recvb,
    bt,
    xs,
    xr,
    acc,
    ys,
    yr,
    own,
    idx,
    load_sem,
    m_send,
    m_recv,
    a_send,
    a_recv,
    x_send,
    x_recv,
    y_send,
    y_recv,
):
    mode = lax.axis_index("mode")
    resp = lax.axis_index("resp")
    core = lax.axis_index("dof")
    me = mode * 2 + core
    x = lax.rem(mode, 4)
    yh = mode // 4
    barrier = pltpu.get_barrier_semaphore()

    def greet(k, carry):
        d = lax.rem(me + k, GROUP)
        pl.semaphore_signal(
            barrier, inc=1, device_id={"mode": d // 2, "dof": lax.rem(d, 2)}
        )
        return carry

    load_p = pltpu.make_async_copy(press_hbm, press, load_sem.at[0])
    load_p.start()
    load_m = pltpu.make_async_copy(modes_hbm, modes.at[core], load_sem.at[1])
    load_m.start()
    lax.fori_loop(1, GROUP, greet, 0)

    def search(d, carry):
        found = jnp.int32(0)
        for j in range(GROUP):
            v = slab[d * GROUP + j]
            found = jnp.where(v // GROUP == me, lax.rem(v, GROUP), found)
        idx[d] = found
        return carry

    lax.fori_loop(0, GROUP, search, 0)
    load_p.wait()

    row = lax.broadcasted_iota(jnp.int32, (96, 96), 0)
    col = lax.broadcasted_iota(jnp.int32, (96, 96), 1)
    hit = jnp.zeros((96, 96), F32)
    for q in range(4):
        i = row - q * BROWS
        hit = hit + jnp.where((i >= 0) & (i < BROWS) & (col == 4 * i + q), 1.0, 0.0)
    pick = hit.astype(BF16)

    def pack(m, carry):
        parts = [
            jnp.dot(pick, press[idx[2 * m + g]], preferred_element_type=F32)
            for g in range(2)
        ]
        for h in range(2):
            for p in range(2):
                q = (h * 2 + p) * BROWS
                sendb[h, 2 * m + p] = jnp.concatenate(
                    [part[q : q + BROWS] for part in parts], axis=0
                ).astype(BF16)
        return carry

    lax.fori_loop(0, CHIPS, pack, 0)
    pl.semaphore_wait(barrier, GROUP - 1)

    for h in range(2):

        def send(k, carry):
            d = lax.rem(me + k, GROUP)
            pltpu.make_async_remote_copy(
                src_ref=sendb.at[h, d],
                dst_ref=recvb.at[h, GROUP - k],
                send_sem=a_send.at[h],
                recv_sem=a_recv.at[h],
                device_id={"mode": d // 2, "dof": lax.rem(d, 2)},
            ).start()
            return carry

        lax.fori_loop(1, GROUP, send, 0)
        if h == 0:
            swap = pltpu.make_async_remote_copy(
                src_ref=modes_hbm,
                dst_ref=modes.at[core],
                send_sem=m_send,
                recv_sem=m_recv,
                device_id={"dof": 1 - core},
            )
            swap.start()
    for h in range(2):
        recvb[h, 0] = sendb[h, me]

    load_m.wait()
    swap.wait()

    def permute(k, carry):
        s = lax.rem(me + k, GROUP)
        at = [jnp.int32(0), jnp.int32(0)]
        for g in range(2):
            for j in range(GROUP):
                v = slab[(2 * mode + g) * GROUP + j]
                at[g] = jnp.where(v // GROUP == s, j, at[g])
        for a in range(CHIPS):
            lanes = pl.ds(a * LANES, LANES)
            perm[a, k] = jnp.concatenate(
                [modes[g, at[g], :, lanes].astype(F32) for g in range(2)], axis=0
            ).astype(BF16)
        return carry

    lax.fori_loop(0, GROUP, permute, 0)

    def x_copy(h, t):
        return pltpu.make_async_remote_copy(
            src_ref=xs.at[h, t],
            dst_ref=xr.at[h, t],
            send_sem=x_send.at[h, t],
            recv_sem=x_recv.at[h, t],
            device_id={"mode": yh * 4 + lax.rem(x + (2, 1, 3)[t], 4)},
        )

    def y_target(k):
        return {
            "mode": lax.rem(yh + k // 2, 4) * 4 + x,
            "dof": lax.rem(core + lax.rem(k, 2), 2),
        }

    def first_stage(h):
        pltpu.make_async_copy(
            recvb.at[h, pl.ds(1, GROUP - 1)],
            recvb.at[h, pl.ds(1, GROUP - 1)],
            a_recv.at[h],
        ).wait()
        bt[...] = recvb[h].reshape(GROUP * 2 * BROWS, LANES).T
        for t, o in enumerate((2, 1, 3, 0)):
            xt = lax.rem(x + o, 4)

            def block(u, carry):
                both = jnp.concatenate(
                    [
                        perm[(2 * u + w) * 4 + xt].reshape(GROUP * 2 * BROWS, LANES)
                        for w in range(2)
                    ],
                    axis=1,
                )
                part = jnp.dot(bt[...], both, preferred_element_type=F32)
                for w in range(2):
                    v = part[:, w * LANES : (w + 1) * LANES]
                    if t == 3:
                        acc[h, 2 * u + w] = v
                    else:
                        xs[h, t, 2 * u + w] = encode(v)
                return carry

            lax.fori_loop(0, 2, block, 0)
            if t < 3:
                x_copy(h, t).start()

    def second_stage(h):
        for t in range(3):
            x_copy(h, t).wait_recv()

        def block(j, carry):
            yt = lax.rem(yh + j, 4)
            total = acc[h, yt]
            for t in range(3):
                total = total + decode(xr[h, t, yt])
            turned = total.T
            for w in range(2):
                half = turned[64 * w : 64 * w + 64]
                ys[h, j, w] = encode(half)
                own[h, j, w] = half
            return carry

        lax.fori_loop(0, 4, block, 0)

        def send(k, carry):
            to = y_target(k)
            pltpu.make_async_remote_copy(
                src_ref=ys.at[h, k // 2, to["dof"]],
                dst_ref=yr.at[h, k],
                send_sem=y_send.at[h],
                recv_sem=y_recv.at[h],
                device_id=to,
            ).start()
            return carry

        lax.fori_loop(1, 8, send, 0)

    def third_stage(h):
        pltpu.make_async_copy(
            yr.at[h, pl.ds(1, 7)], yr.at[h, pl.ds(1, 7)], y_recv.at[h]
        ).wait()
        same = own[h, 0, core]
        other = decode(yr[h, 1])
        for k in range(1, 4):
            same = same + decode(yr[h, 2 * k])
            other = other + decode(yr[h, 2 * k + 1])
        mine = tiles[0:1, :] == mode
        lane = lax.broadcasted_iota(jnp.int32, (64, LANES), 1)
        keep = []
        for b in range(2):
            match = mine & (tiles[1:2, :] == resp * 4 + 2 * h + b)
            keep.append(
                jnp.max(jnp.where(match, 1.0, 0.0), axis=1, keepdims=True)
            )
        mask = jnp.where(lane < 64, keep[0], keep[1])
        same = same * mask
        other = other * mask
        out[pl.ds(2 * h, 64, stride=4), :] = jnp.where(core == 0, same, other)
        out[pl.ds(2 * h + 1, 64, stride=4), :] = jnp.where(core == 0, other, same)

    first_stage(0)
    second_stage(0)
    first_stage(1)
    second_stage(1)
    for h in range(2):
        third_stage(h)

    for h in range(2):
        pltpu.make_async_copy(
            recvb.at[h, pl.ds(1, GROUP - 1)],
            recvb.at[h, pl.ds(1, GROUP - 1)],
            a_send.at[h],
        ).wait()
        for t in range(3):
            x_copy(h, t).wait_send()
        pltpu.make_async_copy(
            yr.at[h, pl.ds(1, 7)], yr.at[h, pl.ds(1, 7)], y_send.at[h]
        ).wait()


def on_device(modes, pressure, tile_list, slab_map):
    rows = pressure.shape[0]
    blocks = rows // BROWS
    press = (
        pressure.reshape(rows, 2, 2, LANES)
        .transpose(0, 2, 1, 3)
        .reshape(blocks, 4 * BROWS, LANES)
    )
    dma = pltpu.SemaphoreType.DMA
    wide = modes.shape[1]
    out = pl.pallas_call(
        kernel,
        out_shape=jax.ShapeDtypeStruct((256, LANES), F32),
        in_specs=[
            pl.BlockSpec(memory_space=pltpu.SMEM),
            pl.BlockSpec(memory_space=pltpu.VMEM),
            pl.BlockSpec(memory_space=pl.ANY),
            pl.BlockSpec(memory_space=pl.ANY),
        ],
        out_specs=pl.BlockSpec(memory_space=pltpu.VMEM),
        scratch_shapes=[
            pltpu.VMEM((blocks, 4 * BROWS, LANES), BF16),
            pltpu.VMEM((2, blocks, BROWS, wide), BF16),
            pltpu.VMEM((CHIPS, GROUP, 2 * BROWS, LANES), BF16),
            pltpu.VMEM((2, GROUP, 2 * BROWS, LANES), BF16),
            pltpu.VMEM((2, GROUP, 2 * BROWS, LANES), BF16),
            pltpu.VMEM((LANES, GROUP * 2 * BROWS), BF16),
            pltpu.VMEM((2, 3, 4, 144, LANES), I16),
            pltpu.VMEM((2, 3, 4, 144, LANES), I16),
            pltpu.VMEM((2, 4, LANES, LANES), F32),
            pltpu.VMEM((2, 4, 2, 80, LANES), I16),
            pltpu.VMEM((2, 8, 80, LANES), I16),
            pltpu.VMEM((2, 4, 2, 64, LANES), F32),
            pltpu.SMEM((GROUP,), jnp.int32),
            dma((2,)),
            dma,
            dma,
            dma((2,)),
            dma((2,)),
            dma((2, 3)),
            dma((2, 3)),
            dma((2,)),
            dma((2,)),
        ],
        compiler_params=pltpu.CompilerParams(
            collective_id=0, has_side_effects=True, vmem_limit_bytes=40 << 20
        ),
        name="forces",
    )(
        slab_map,
        tile_list.T,
        press,
        modes.reshape(blocks, BROWS, wide),
    )
    return (
        out.reshape(64, 2, 2, LANES).transpose(0, 2, 1, 3).reshape(64, 2, 2 * LANES)
    )


def solution(mesh):
    return jax.shard_map(
        on_device,
        mesh=mesh,
        in_specs=(P(("mode", "dof"), None), P(("mode", "dof"), None, "resp"), P(), P()),
        out_specs=P(("mode", "dof"), None, "resp"),
        check_vma=False,
    )
```

time: 179 us -> 65.6 us (0.37)
  waiting for transfers between devices: 126 us -> 0 us
  Pallas kernels: 0 us -> 60.3 us
  between operations: 13.5 us -> 0.01 us
  local copies, waits for them, and re-layouts: 16.7 us -> 5.05 us
  starting transfers between devices: 11.3 us -> 0 us
  other arithmetic: 6.41 us -> 0 us
  matrix products: 3.97 us -> 0 us
    unnamed x2 -> x0, waiting for transfers between devices: 106 us -> none
    pallas_call x0 -> x1, Pallas kernels: none -> 60.3 us  [on_device(): pl.pallas_call(kernel, out_shape=jax.ShapeDtypeStruct((256, LANES), F32),...]
    all_to_all x1 -> x0, waiting for transfers between devices: 20.5 us -> none  [on_device(): lax.all_to_all(outgoing, ('mode', 'dof'), split_axis=0, concat_axis=0, ti...]
    all_to_all x1 -> x0, starting transfers between devices: 11.3 us -> none  [on_device(): lax.all_to_all(outgoing, ('mode', 'dof'), split_axis=0, concat_axis=0, ti...]
    gather x2 -> x0, local copies, waits for them, and re-layouts: 5.27 us -> none  [the longest x1 2.63 us: on_device(): jnp.take(received, own_source, axis=0).reshape(dof_rows, 2 * resp_cols)]
    reshape x3 -> x0, local copies, waits for them, and re-layouts: 4.84 us -> none  [the longest x1 3.14 us: on_device(): blocks = pressure.reshape(group_size, block_rows, 2 * resp_cols)]
    dot_general x1 -> x0, matrix products: 3.97 us -> none  [on_device(): lax.dot_general(modes, aligned, (((0,), (0,)), ((), ())), preferred_eleme...]
    select_n x5 -> x0, other arithmetic: 3.58 us -> none  [the longest x2 2.18 us: on_device(): outgoing = jnp.take(blocks, send_index, axis=0)]
  transfers between devices with their start and end apart: 2 -> 0, of which waited for: 2 -> 0; matrix products, arithmetic and copies ran while one was open for 2% -> 0% of each run, Pallas kernels for 0% -> 0%
where the time goes in v1:
time: 65.6 us; the launch traced here: 65.4 us
  Pallas kernels  60.3 us (92%)
  local copies, waits for them, and re-layouts  5.05 us (8%)
    pallas_call x1, Pallas kernels, on_device(): pl.pallas_call(kernel, out_shape=jax.ShapeDtypeStruct((256, LANES), F32),...  60.3 us
    unnamed x9, local copies, waits for them, and re-layouts  5.05 us

profile of v1, /device:TPU:1, one launch (start us, length us, event | category | flops | bytes accessed | tf_op | source)
XLA Modules:
  0.0 65.4 jit_solution(1514702565056955942)
XLA Ops:
  0.0 0.0 copy-start
  0.0 1.9 %copy-done = bf16[768,2048]{1,0:T(8,128)(2,1)S(1)} copy-done((bf16[768,2048]{1,0:T(8,128)(2,1)S(1)}, bf16[768,2048]{1,0:T(8,128)(2,1)}, u32[]{:S(2)}) %copy-start) | copy-done | bytes 3145752
  1.9 0.0 copy-start.1
  1.9 1.1 %copy-done.1 = bf16[768,2,256]{2,1,0:T(2,128)(2,1)S(1)} copy-done((bf16[768,2,256]{2,1,0:T(2,128)(2,1)S(1)}, bf16[768,2,256]{2,1,0:T(2,128)(2,1)}, u32[]{:S(2)}) %copy-start.1) | copy-done | bytes 786456
  3.0 0.0 copy-start.2
  3.0 0.7 %copy-done.2 = s32[640,2]{0,1:T(2,128)S(1)} copy-done((s32[640,2]{0,1:T(2,128)S(1)}, s32[640,2]{0,1:T(2,128)}, u32[]{:S(2)}) %copy-start.2) | copy-done | bytes 5144
  3.7 0.0 copy-start.3
  3.7 0.7 %copy-done.3 = s32[1024]{0:T(1024)S(1)} copy-done((s32[1024]{0:T(1024)S(1)}, s32[1024]{0:T(1024)}, u32[]{:S(2)}) %copy-start.3) | copy-done | bytes 4120
  4.4 60.3 %forces.1 = f32[256,128]{1,0:T(8,128)S(1)} custom-call(s32[1024]{0:T(1024)S(1)} %copy-done.3, s32[2,640]{1,0:T(2,128)S(1)} %bitcast.15, bf16[32,96,128]{2,1,0:T(8,128)(2,1)S(1)} %bitcast.13, bf16[32,24,2048]{2,1,0:T(8,128)(2,1)S(1)} %bitcast.12), custom_call_target="tpu_custom_call" | custom-call | tf_op jit(solution)/shard_map/forces/pallas_call | solution.py:298
  64.7 0.7 %copy.8 = f32[64,2,256]{2,1,0:T(2,128)} copy(f32[64,2,256]{2,1,0:T(2,128)S(1)} %bitcast.14) | data formatting | bytes 262144
Async XLA Ops:
  0.0 1.9 %copy-start = (bf16[768,2048]{1,0:T(8,128)(2,1)S(1)}, bf16[768,2048]{1,0:T(8,128)(2,1)}, u32[]{:S(2)}) copy-start(bf16[768,2048]{1,0:T(8,128)(2,1)} %param.4) | copy-start | bytes 9437188
  1.9 1.1 %copy-start.1 = (bf16[768,2,256]{2,1,0:T(2,128)(2,1)S(1)}, bf16[768,2,256]{2,1,0:T(2,128)(2,1)}, u32[]{:S(2)}) copy-start(bf16[768,2,256]{2,1,0:T(2,128)(2,1)} %param.5) | copy-start | bytes 2359300
  3.0 0.7 %copy-start.2 = (s32[640,2]{0,1:T(2,128)S(1)}, s32[640,2]{0,1:T(2,128)}, u32[]{:S(2)}) copy-start(s32[640,2]{0,1:T(2,128)} %param.6) | copy-start | bytes 15364
  3.7 0.7 %copy-start.3 = (s32[1024]{0:T(1024)S(1)}, s32[1024]{0:T(1024)}, u32[]{:S(2)}) copy-start(s32[1024]{0:T(1024)} %slab.1) | copy-start | bytes 12292

commit v2 on v1

v2 whole, which is shorter than its diff:
```python
import functools

import jax
import jax.numpy as jnp
from jax import lax
from jax.experimental import pallas as pl
from jax.experimental.pallas import tpu as pltpu
from jax.sharding import PartitionSpec as P

F32 = jnp.float32
BF16 = jnp.bfloat16
I16 = jnp.int16
LANES = 128
BROWS = 24
GROUP = 32
CHIPS = 16
TOP = 32760.0
STEP = 64.0


def encode(v):
    r = v.shape[0]
    v3 = v.reshape(r // 16, 16, LANES)
    top = jnp.maximum(jnp.max(jnp.abs(v3), axis=0), 2.0**-110)
    e = jnp.ceil(jnp.log2(top) * STEP)
    inv = jnp.exp2(e * (-1.0 / STEP)) * TOP
    code = jnp.round(v3 * inv[None]).astype(jnp.int32).reshape(r, LANES)
    return jnp.concatenate([code, e.astype(jnp.int32)], axis=0).astype(I16)


def decode(q):
    r = q.shape[0] - 16
    w = q.astype(jnp.int32).astype(F32)
    scale = jnp.exp2(w[r:] * (1.0 / STEP)) * (1.0 / TOP)
    return (w[:r].reshape(r // 16, 16, LANES) * scale[None]).reshape(r, LANES)


def kernel(
    slab_hbm,
    slabv_hbm,
    tiles_hbm,
    press_hbm,
    modes_hbm,
    out,
    slab,
    slabv,
    found,
    table,
    tiles,
    press,
    modes,
    bal,
    sendb,
    recv0,
    recv1,
    bt,
    xs,
    xr,
    acc,
    ys,
    yr,
    own,
    pick,
    load_sem,
    m_send,
    m_recv,
    a_send,
    a_recv,
    x_send,
    x_recv,
    y_send,
    y_recv,
):
    mode = lax.axis_index("mode")
    resp = lax.axis_index("resp")
    core = lax.axis_index("dof")
    me = mode * 2 + core
    x = lax.rem(mode, 4)
    yh = mode // 4
    barrier = pltpu.get_barrier_semaphore()

    def greet(k, carry):
        d = lax.rem(me + k, GROUP)
        pl.semaphore_signal(
            barrier, inc=1, device_id={"mode": d // 2, "dof": lax.rem(d, 2)}
        )
        return carry

    load_v = pltpu.make_async_copy(slabv_hbm, slabv, load_sem.at[4])
    load_v.start()
    load_s = pltpu.make_async_copy(slab_hbm, slab, load_sem.at[2])
    load_s.start()
    load_p = pltpu.make_async_copy(press_hbm, press, load_sem.at[0])
    load_p.start()
    load_m = pltpu.make_async_copy(modes_hbm, modes.at[core], load_sem.at[1])
    load_m.start()
    load_t = pltpu.make_async_copy(tiles_hbm, tiles, load_sem.at[3])
    load_t.start()
    lax.fori_loop(1, GROUP, greet, 0)

    load_v.wait()
    ids = slabv[...]
    local = jnp.where(ids // GROUP == me, lax.rem(ids, GROUP), 0)
    for shift in (1, 2, 4, 8, 16):
        local = local + pltpu.roll(local, LANES - shift, 1)
    found[...] = lax.rem(local, GROUP)
    to_smem = pltpu.make_async_copy(found, table, load_sem.at[5])
    to_smem.start()

    row = lax.broadcasted_iota(jnp.int32, (96, 96), 0)
    col = lax.broadcasted_iota(jnp.int32, (96, 96), 1)
    hit = jnp.zeros((96, 96), F32)
    for q in range(4):
        i = row - q * BROWS
        hit = hit + jnp.where((i >= 0) & (i < BROWS) & (col == 4 * i + q), 1.0, 0.0)
    pick[...] = hit.astype(BF16)

    def a_copy(h, d):
        return pltpu.make_async_remote_copy(
            src_ref=sendb.at[h, d],
            dst_ref=(recv0, recv1)[h].at[lax.rem(me - d + GROUP, GROUP)],
            send_sem=a_send.at[h],
            recv_sem=a_recv.at[h],
            device_id={"mode": d // 2, "dof": lax.rem(d, 2)},
        )

    def a_wait(sem):
        part = recv0.at[pl.ds(1, GROUP - 1)]
        pltpu.make_async_copy(part, part, sem).wait()

    load_s.wait()
    load_p.wait()
    to_smem.wait()
    pl.semaphore_wait(barrier, GROUP - 1)
    swap = pltpu.make_async_remote_copy(
        src_ref=modes_hbm,
        dst_ref=modes.at[core],
        send_sem=m_send,
        recv_sem=m_recv,
        device_id={"dof": 1 - core},
    )
    swap.start()

    def pack(m):
        parts = []
        for g in range(2):
            d = 2 * m + g
            block = press[table[d // 4, GROUP * lax.rem(d, 4)]]
            parts.append(jnp.dot(pick[...], block, preferred_element_type=F32))
        for h in range(2):
            for p in range(2):
                q = (h * 2 + p) * BROWS
                sendb[h, 2 * m + p] = jnp.concatenate(
                    [part[q : q + BROWS] for part in parts], axis=0
                ).astype(BF16)

    def chip(k):
        r = lax.rem(k, 3)
        step = jnp.where(r == 0, 2, jnp.where(r == 1, 1, 3))
        far = k < 12
        dy = jnp.where(far, step, 0)
        dx = jnp.where(far, k // 3, step)
        return lax.rem(yh + dy, 4) * 4 + lax.rem(x + dx, 4)

    def pack_and_send(k, carry):
        m = chip(k)
        pack(m)
        for p in range(2):
            a_copy(0, 2 * m + p).start()
        return carry

    lax.fori_loop(0, CHIPS - 1, pack_and_send, 0, unroll=3)
    pack(mode)
    mate = mode * 2 + 1 - core
    recv0[0] = sendb[0, me]
    recv1[0] = sendb[1, me]
    a_copy(0, mate).start()

    a_wait(a_send.at[0])

    def send(k, carry):
        for p in range(2):
            a_copy(1, 2 * chip(k) + p).start()
        return carry

    lax.fori_loop(0, CHIPS - 1, send, 0)
    a_copy(1, mate).start()
    load_m.wait()
    swap.wait()

    def across(t):
        return jnp.where(t == 0, 2, jnp.where(t == 1, 1, jnp.where(t == 2, 3, 0)))

    def x_copy(h, t):
        return pltpu.make_async_remote_copy(
            src_ref=xs.at[h, t],
            dst_ref=xr.at[h, t],
            send_sem=x_send.at[h, t],
            recv_sem=x_recv.at[h, t],
            device_id={"mode": yh * 4 + lax.rem(x + across(t), 4)},
        )

    def y_wait(sem):
        part = yr.at[0, pl.ds(1, 7)]
        pltpu.make_async_copy(part, part, sem).wait()

    def first_stage(h):
        a_wait(a_recv.at[h])

        def align(recv, i, carry):
            for g in range(2):
                parts = []
                for w in range(2):
                    q = slab[(2 * mode + g) * GROUP + 2 * i + w] // GROUP
                    slot = lax.rem(q - me + GROUP, GROUP)
                    both = recv[slot].astype(F32)
                    parts.append(both[g * BROWS : (g + 1) * BROWS])
                bal[g, i] = jnp.concatenate(parts, axis=0).astype(BF16)
            return carry

        for way, recv in enumerate((recv0, recv1)):

            @pl.when(h == way)
            def _():
                lax.fori_loop(0, GROUP // 2, functools.partial(align, recv), 0)

        bt[...] = bal[...].reshape(GROUP * 2 * BROWS, LANES).T

        def block(n, carry):
            t = n // 2
            u = lax.rem(n, 2)
            xt = lax.rem(x + across(t), 4)
            part = jnp.zeros((LANES, 2 * LANES), F32)
            for g in range(2):
                both = jnp.concatenate(
                    [
                        modes[g, :, pl.ds(((2 * u + w) * 4 + xt) * LANES, LANES)]
                        for w in range(2)
                    ],
                    axis=1,
                )
                depth = GROUP * BROWS
                part = part + jnp.dot(
                    bt[:, g * depth : (g + 1) * depth],
                    both,
                    preferred_element_type=F32,
                )
            halves = [part[:, w * LANES : (w + 1) * LANES] for w in range(2)]

            @pl.when(t == 3)
            def _():
                for w in range(2):
                    acc[h, 2 * u + w] = halves[w]

            @pl.when(t < 3)
            def _():
                for w in range(2):
                    xs[h, t, 2 * u + w] = encode(halves[w])

                @pl.when(u == 1)
                def _():
                    x_copy(h, t).start()

            return carry

        lax.fori_loop(0, 8, block, 0)

    def second_stage(h):
        for t in range(3):
            x_copy(h, t).wait_recv()

        def block(j, carry):
            yt = lax.rem(yh + j, 4)
            total = acc[h, yt]
            for t in range(3):
                total = total + decode(xr[h, t, yt])
            turned = total.T

            @pl.when(j == 0)
            def _():
                own[h] = turned.reshape(2, 64, LANES)

            for w in range(2):
                ys[h, j, w] = encode(turned[64 * w : 64 * w + 64])

            def send(w, carry):
                to = lax.rem(core + w, 2)
                pltpu.make_async_remote_copy(
                    src_ref=ys.at[h, j, to],
                    dst_ref=yr.at[h, 2 * j + w],
                    send_sem=y_send.at[h],
                    recv_sem=y_recv.at[h],
                    device_id={"mode": yt * 4 + x, "dof": to},
                ).start()
                return carry

            lax.fori_loop(jnp.where(j == 0, 1, 0), 2, send, 0)
            return carry

        lax.fori_loop(0, 4, block, 0)

    def third_stage(h):
        y_wait(y_recv.at[h])
        same = own[h, core]
        other = decode(yr[h, 1])
        for k in range(1, 4):
            same = same + decode(yr[h, 2 * k])
            other = other + decode(yr[h, 2 * k + 1])
        mine = tiles[0:1, :] == mode
        lane = lax.broadcasted_iota(jnp.int32, (64, LANES), 1)
        keep = []
        for b in range(2):
            match = mine & (tiles[1:2, :] == resp * 4 + 2 * h + b)
            keep.append(jnp.max(jnp.where(match, 1.0, 0.0), axis=1, keepdims=True))
        mask = jnp.where(lane < 64, keep[0], keep[1])
        same = same * mask
        other = other * mask
        out[pl.ds(2 * h, 64, stride=4), :] = jnp.where(core == 0, same, other)
        out[pl.ds(2 * h + 1, 64, stride=4), :] = jnp.where(core == 0, other, same)

    def first(h, carry):
        first_stage(h)
        return carry

    def second(h, carry):
        second_stage(h)
        return carry

    def third(h, carry):
        third_stage(h)
        return carry

    lax.fori_loop(0, 2, first, 0)
    lax.fori_loop(0, 2, second, 0)
    load_t.wait()
    lax.fori_loop(0, 2, third, 0)

    a_wait(a_send.at[1])
    for h in range(2):
        for t in range(3):
            x_copy(h, t).wait_send()
        y_wait(y_send.at[h])


def on_device(modes, pressure, tile_list, slab_map):
    rows = pressure.shape[0]
    blocks = rows // BROWS
    press = (
        pressure.reshape(rows, 2, 2, LANES)
        .transpose(0, 2, 1, 3)
        .reshape(blocks, 4 * BROWS, LANES)
    )
    dma = pltpu.SemaphoreType.DMA
    wide = modes.shape[1]
    out = pl.pallas_call(
        kernel,
        out_shape=jax.ShapeDtypeStruct((256, LANES), F32),
        in_specs=[
            pl.BlockSpec(memory_space=pltpu.HBM),
            pl.BlockSpec(memory_space=pltpu.HBM),
            pl.BlockSpec(memory_space=pltpu.HBM),
            pl.BlockSpec(memory_space=pltpu.HBM),
            pl.BlockSpec(memory_space=pltpu.HBM),
        ],
        out_specs=pl.BlockSpec(memory_space=pltpu.VMEM),
        scratch_shapes=[
            pltpu.SMEM(slab_map.shape, jnp.int32),
            pltpu.VMEM((8, LANES), jnp.int32),
            pltpu.VMEM((8, LANES), jnp.int32),
            pltpu.SMEM((8, LANES), jnp.int32),
            pltpu.VMEM(tile_list.shape[::-1], jnp.int32),
            pltpu.VMEM((blocks, 4 * BROWS, LANES), BF16),
            pltpu.VMEM((2, rows, wide), BF16),
            pltpu.VMEM((2, blocks // 2, 2 * BROWS, LANES), BF16),
            pltpu.VMEM((2, GROUP, 2 * BROWS, LANES), BF16),
            pltpu.VMEM((GROUP, 2 * BROWS, LANES), BF16),
            pltpu.VMEM((GROUP, 2 * BROWS, LANES), BF16),
            pltpu.VMEM((LANES, GROUP * 2 * BROWS), BF16),
            pltpu.VMEM((2, 3, 4, 144, LANES), I16),
            pltpu.VMEM((2, 3, 4, 144, LANES), I16),
            pltpu.VMEM((2, 4, LANES, LANES), F32),
            pltpu.VMEM((2, 4, 2, 80, LANES), I16),
            pltpu.VMEM((2, 8, 80, LANES), I16),
            pltpu.VMEM((2, 2, 64, LANES), F32),
            pltpu.VMEM((96, 96), BF16),
            dma((6,)),
            dma,
            dma,
            dma((2,)),
            dma((2,)),
            dma((2, 3)),
            dma((2, 3)),
            dma((2,)),
            dma((2,)),
        ],
        compiler_params=pltpu.CompilerParams(
            collective_id=0, has_side_effects=True, vmem_limit_bytes=60 << 20
        ),
        name="forces",
    )(
        slab_map,
        slab_map.reshape(8, LANES),
        tile_list.T,
        press,
        modes,
    )
    return (
        out.reshape(64, 2, 2, LANES).transpose(0, 2, 1, 3).reshape(64, 2, 2 * LANES)
    )


def solution(mesh):
    return jax.shard_map(
        on_device,
        mesh=mesh,
        in_specs=(P(("mode", "dof"), None), P(("mode", "dof"), None, "resp"), P(), P()),
        out_specs=P(("mode", "dof"), None, "resp"),
        check_vma=False,
    )
```

time: 65.6 us -> 55.4 us (0.84)
  Pallas kernels: 60.3 us -> 53.7 us
  local copies, waits for them, and re-layouts: 5.05 us -> 1.57 us
    pallas_call x1, Pallas kernels: 60.3 us -> 53.7 us  [on_device(): pl.pallas_call(kernel, out_shape=jax.ShapeDtypeStruct((256, LANES), F32),...]
    unnamed x9 -> x1, local copies, waits for them, and re-layouts: 5.05 us -> 1.57 us
where the time goes in v2:
time: 55.4 us; the launch traced here: 55.2 us
  Pallas kernels  53.7 us (97%)
  local copies, waits for them, and re-layouts  1.57 us (3%)
    pallas_call x1, Pallas kernels, on_device(): pl.pallas_call(kernel, out_shape=jax.ShapeDtypeStruct((256, LANES), F32),...  53.7 us
    unnamed x1, local copies, waits for them, and re-layouts  1.57 us

profile of v2, /device:TPU:1, one launch (start us, length us, event | category | flops | bytes accessed | tf_op | source)
XLA Modules:
  0.0 55.2 jit_solution(4462904060582997773)
XLA Ops:
  0.0 53.7 %forces.1 = f32[256,128]{1,0:T(8,128)} custom-call(s32[1024]{0:T(1024)} %slab_hbm.1, s32[8,128]{1,0:T(8,128)} %bitcast.14, s32[2,640]{1,0:T(2,128)} %bitcast.15, bf16[32,96,128]{2,1,0:T(8,128)(2,1)} %bitcast.12, bf16[768,2048]{1,0:T(8,128)(2,1)} %modes_hbm.1), custom_call_target="tpu_custom_call" | custom-call | tf_op jit(solution)/shard_map/forces/pallas_call | solution.py:355
  53.7 1.6 %copy.8 = f32[64,2,256]{2,1,0:T(2,128)} copy(f32[64,2,256]{2,1,0:T(2,128)} %bitcast.13) | data formatting | bytes 262144

commit v3 on v2

--- a/solution.py
+++ b/solution.py
@@ -176,8 +176,6 @@
     recv1[0] = sendb[1, me]
     a_copy(0, mate).start()
 
-    a_wait(a_send.at[0])
-
     def send(k, carry):
         for p in range(2):
             a_copy(1, 2 * chip(k) + p).start()
@@ -191,12 +189,12 @@
     def across(t):
         return jnp.where(t == 0, 2, jnp.where(t == 1, 1, jnp.where(t == 2, 3, 0)))
 
-    def x_copy(h, t):
+    def x_copy(h, t, u):
         return pltpu.make_async_remote_copy(
-            src_ref=xs.at[h, t],
-            dst_ref=xr.at[h, t],
-            send_sem=x_send.at[h, t],
-            recv_sem=x_recv.at[h, t],
+            src_ref=xs.at[h, t, u],
+            dst_ref=xr.at[h, t, u],
+            send_sem=x_send.at[h, t, u],
+            recv_sem=x_recv.at[h, t, u],
             device_id={"mode": yh * 4 + lax.rem(x + across(t), 4)},
         )
 
@@ -227,8 +225,8 @@
         bt[...] = bal[...].reshape(GROUP * 2 * BROWS, LANES).T
 
         def block(n, carry):
-            t = n // 2
-            u = lax.rem(n, 2)
+            u = n // 4
+            t = lax.rem(n, 4)
             xt = lax.rem(x + across(t), 4)
             part = jnp.zeros((LANES, 2 * LANES), F32)
             for g in range(2):
@@ -255,25 +253,23 @@
             @pl.when(t < 3)
             def _():
                 for w in range(2):
-                    xs[h, t, 2 * u + w] = encode(halves[w])
-
-                @pl.when(u == 1)
-                def _():
-                    x_copy(h, t).start()
+                    xs[h, t, u, w] = encode(halves[w])
+                x_copy(h, t, u).start()
 
             return carry
 
         lax.fori_loop(0, 8, block, 0)
 
-    def second_stage(h):
+    def second_stage(h, u):
         for t in range(3):
-            x_copy(h, t).wait_recv()
-
-        def block(j, carry):
-            yt = lax.rem(yh + j, 4)
+            x_copy(h, t, u).wait_recv()
+
+        def block(v, carry):
+            yt = 2 * u + v
+            j = lax.rem(yt - yh + 4, 4)
             total = acc[h, yt]
             for t in range(3):
-                total = total + decode(xr[h, t, yt])
+                total = total + decode(xr[h, t, u, v])
             turned = total.T
 
             @pl.when(j == 0)
@@ -297,7 +293,7 @@
             lax.fori_loop(jnp.where(j == 0, 1, 0), 2, send, 0)
             return carry
 
-        lax.fori_loop(0, 4, block, 0)
+        lax.fori_loop(0, 2, block, 0)
 
     def third_stage(h):
         y_wait(y_recv.at[h])
@@ -322,8 +318,8 @@
         first_stage(h)
         return carry
 
-    def second(h, carry):
-        second_stage(h)
+    def second(n, carry):
+        second_stage(n // 2, lax.rem(n, 2))
         return carry
 
     def third(h, carry):
@@ -331,14 +327,16 @@
         return carry
 
     lax.fori_loop(0, 2, first, 0)
-    lax.fori_loop(0, 2, second, 0)
+    lax.fori_loop(0, 4, second, 0)
     load_t.wait()
     lax.fori_loop(0, 2, third, 0)
 
+    a_wait(a_send.at[0])
     a_wait(a_send.at[1])
     for h in range(2):
         for t in range(3):
-            x_copy(h, t).wait_send()
+            for u in range(2):
+                x_copy(h, t, u).wait_send()
         y_wait(y_send.at[h])
 
 
@@ -376,8 +374,8 @@
             pltpu.VMEM((GROUP, 2 * BROWS, LANES), BF16),
             pltpu.VMEM((GROUP, 2 * BROWS, LANES), BF16),
             pltpu.VMEM((LANES, GROUP * 2 * BROWS), BF16),
-            pltpu.VMEM((2, 3, 4, 144, LANES), I16),
-            pltpu.VMEM((2, 3, 4, 144, LANES), I16),
+            pltpu.VMEM((2, 3, 2, 2, 144, LANES), I16),
+            pltpu.VMEM((2, 3, 2, 2, 144, LANES), I16),
             pltpu.VMEM((2, 4, LANES, LANES), F32),
             pltpu.VMEM((2, 4, 2, 80, LANES), I16),
             pltpu.VMEM((2, 8, 80, LANES), I16),
@@ -388,8 +386,8 @@
             dma,
             dma((2,)),
             dma((2,)),
-            dma((2, 3)),
-            dma((2, 3)),
+            dma((2, 3, 2)),
+            dma((2, 3, 2)),
             dma((2,)),
             dma((2,)),
         ],

time: 55.4 us -> 50.5 us (0.912)
  Pallas kernels: 53.7 us -> 48.7 us
    pallas_call x1, Pallas kernels: 53.7 us -> 48.7 us  [on_device(): pl.pallas_call(kernel, out_shape=jax.ShapeDtypeStruct((256, LANES), F32),...]
where the time goes in v3:
time: 50.5 us; the launch traced here: 50.3 us
  Pallas kernels  48.7 us (96%)
  local copies, waits for them, and re-layouts  1.57 us (3%)
    pallas_call x1, Pallas kernels, on_device(): pl.pallas_call(kernel, out_shape=jax.ShapeDtypeStruct((256, LANES), F32),...  48.7 us
    unnamed x1, local copies, waits for them, and re-layouts  1.57 us

profile of v3, /device:TPU:1, one launch (start us, length us, event | category | flops | bytes accessed | tf_op | source)
XLA Modules:
  0.0 50.3 jit_solution(3683060957026700370)
XLA Ops:
  0.0 48.7 %forces.1 = f32[256,128]{1,0:T(8,128)} custom-call(s32[1024]{0:T(1024)} %slab_hbm.1, s32[8,128]{1,0:T(8,128)} %bitcast.14, s32[2,640]{1,0:T(2,128)} %bitcast.15, bf16[32,96,128]{2,1,0:T(8,128)(2,1)} %bitcast.12, bf16[768,2048]{1,0:T(8,128)(2,1)} %modes_hbm.1), custom_call_target="tpu_custom_call" | custom-call | tf_op jit(solution)/shard_map/forces/pallas_call | solution.py:353
  48.8 1.6 %copy.8 = f32[64,2,256]{2,1,0:T(2,128)} copy(f32[64,2,256]{2,1,0:T(2,128)} %bitcast.13) | data formatting | bytes 262144

commit v4 on v3

--- a/solution.py
+++ b/solution.py
@@ -159,7 +159,7 @@
         step = jnp.where(r == 0, 2, jnp.where(r == 1, 1, 3))
         far = k < 12
         dy = jnp.where(far, step, 0)
-        dx = jnp.where(far, k // 3, step)
+        dx = jnp.where(far, lax.rem(core * 2 + k // 3, 4), step)
         return lax.rem(yh + dy, 4) * 4 + lax.rem(x + dx, 4)
 
     def pack_and_send(k, carry):
@@ -187,7 +187,7 @@
     swap.wait()
 
     def across(t):
-        return jnp.where(t == 0, 2, jnp.where(t == 1, 1, jnp.where(t == 2, 3, 0)))
+        return jnp.where(t == 0, 1, jnp.where(t == 1, 3, jnp.where(t == 2, 2, 0)))
 
     def x_copy(h, t, u):
         return pltpu.make_async_remote_copy(

time: 50.5 us -> 49.9 us (0.988)
    pallas_call x1, Pallas kernels: 48.7 us -> 48.2 us  [on_device(): pl.pallas_call(kernel, out_shape=jax.ShapeDtypeStruct((256, LANES), F32),...]
where the time goes in v4:
time: 49.9 us; the launch traced here: 49.8 us
  Pallas kernels  48.2 us (97%)
  local copies, waits for them, and re-layouts  1.57 us (3%)
    pallas_call x1, Pallas kernels, on_device(): pl.pallas_call(kernel, out_shape=jax.ShapeDtypeStruct((256, LANES), F32),...  48.2 us
    unnamed x1, local copies, waits for them, and re-layouts  1.57 us

profile of v4, /device:TPU:1, one launch (start us, length us, event | category | flops | bytes accessed | tf_op | source)
XLA Modules:
  0.0 49.8 jit_solution(12281874651760495899)
XLA Ops:
  0.0 48.2 %forces.1 = f32[256,128]{1,0:T(8,128)} custom-call(s32[1024]{0:T(1024)} %slab_hbm.1, s32[8,128]{1,0:T(8,128)} %bitcast.14, s32[2,640]{1,0:T(2,128)} %bitcast.15, bf16[32,96,128]{2,1,0:T(8,128)(2,1)} %bitcast.12, bf16[768,2048]{1,0:T(8,128)(2,1)} %modes_hbm.1), custom_call_target="tpu_custom_call" | custom-call | tf_op jit(solution)/shard_map/forces/pallas_call | solution.py:353
  48.2 1.6 %copy.8 = f32[64,2,256]{2,1,0:T(2,128)} copy(f32[64,2,256]{2,1,0:T(2,128)} %bitcast.13) | data formatting | bytes 262144

commit v5 on v4

--- a/solution.py
+++ b/solution.py
@@ -293,15 +293,9 @@
             lax.fori_loop(jnp.where(j == 0, 1, 0), 2, send, 0)
             return carry
 
-        lax.fori_loop(0, 2, block, 0)
+        lax.fori_loop(0, 2, block, 0, unroll=True)
 
     def third_stage(h):
-        y_wait(y_recv.at[h])
-        same = own[h, core]
-        other = decode(yr[h, 1])
-        for k in range(1, 4):
-            same = same + decode(yr[h, 2 * k])
-            other = other + decode(yr[h, 2 * k + 1])
         mine = tiles[0:1, :] == mode
         lane = lax.broadcasted_iota(jnp.int32, (64, LANES), 1)
         keep = []
@@ -309,6 +303,12 @@
             match = mine & (tiles[1:2, :] == resp * 4 + 2 * h + b)
             keep.append(jnp.max(jnp.where(match, 1.0, 0.0), axis=1, keepdims=True))
         mask = jnp.where(lane < 64, keep[0], keep[1])
+        y_wait(y_recv.at[h])
+        same = own[h, core]
+        other = decode(yr[h, 1])
+        for k in range(1, 4):
+            same = same + decode(yr[h, 2 * k])
+            other = other + decode(yr[h, 2 * k + 1])
         same = same * mask
         other = other * mask
         out[pl.ds(2 * h, 64, stride=4), :] = jnp.where(core == 0, same, other)

time: 49.9 us -> 49.9 us (level)
  no operation moved by 1% of the time
where the time goes in v5:
time: 49.9 us; the launch traced here: 49.8 us
  Pallas kernels  48.2 us (97%)
  local copies, waits for them, and re-layouts  1.57 us (3%)
    pallas_call x1, Pallas kernels, on_device(): pl.pallas_call(kernel, out_shape=jax.ShapeDtypeStruct((256, LANES), F32),...  48.2 us
    unnamed x1, local copies, waits for them, and re-layouts  1.57 us

profile of v5, /device:TPU:1, one launch (start us, length us, event | category | flops | bytes accessed | tf_op | source)
XLA Modules:
  0.0 49.8 jit_solution(3434554957688215805)
XLA Ops:
  0.0 48.2 %forces.1 = f32[256,128]{1,0:T(8,128)} custom-call(s32[1024]{0:T(1024)} %slab_hbm.1, s32[8,128]{1,0:T(8,128)} %bitcast.14, s32[2,640]{1,0:T(2,128)} %bitcast.15, bf16[32,96,128]{2,1,0:T(8,128)(2,1)} %bitcast.12, bf16[768,2048]{1,0:T(8,128)(2,1)} %modes_hbm.1), custom_call_target="tpu_custom_call" | custom-call | tf_op jit(solution)/shard_map/forces/pallas_call | solution.py:353
  48.2 1.6 %copy.8 = f32[64,2,256]{2,1,0:T(2,128)} copy(f32[64,2,256]{2,1,0:T(2,128)} %bitcast.13) | data formatting | bytes 262144
